TPU v7x, 32 devices: a whole 2x2x4 slice. The times are simulated.
32 devices in a mesh: expert: 4 (over y, x), dp: 8 (over z, core).
Axes of the slice: x: 2, y: 2, z: 4, core: 2. Of those that a mesh axis runs over, the one named last changes fastest.
Arguments:
- inputs: bfloat16 [32768, 768], P(('expert', 'dp')), may hold values from -6 to 6
- gain_attn: bfloat16 [768], P('dp'), may hold values from 0.5 to 1.5
- w_query: bfloat16 [768, 768], P('dp'), may hold values from -0.109375 to 0.109375
- w_key: bfloat16 [768, 768], P('dp'), may hold values from -0.109375 to 0.109375
- w_value: bfloat16 [768, 768], P('dp'), may hold values from -0.21875 to 0.21875
- w_output: bfloat16 [768, 768], P('dp'), may hold values from -0.875 to 0.875
- bias_table: bfloat16 [32, 12], P('dp'), may hold values from -6 to 6
- gain_ffn: bfloat16 [768], P('dp'), may hold values from 0.5 to 1.5
- w_router: bfloat16 [768, 32], P('dp'), may hold values from -0.109375 to 0.109375
- w_in: bfloat16 [32, 3072, 768], P('expert'), may hold values from -0.21875 to 0.21875
- w_out: bfloat16 [32, 3072, 768], P('expert'), may hold values from -4 to 4
- segments: int32 [32, 1024], P(('expert', 'dp')), may hold values from 0 to 3, never falling along the last dimension, each value on 1 to 512 neighbouring positions
- buckets: int32 [1024, 1024], replicated, may hold values from 0 to 31, as said below
- routes: int32 [32768], P(('expert', 'dp')), may hold values from 0 to 31, as said below
- slot_ids: int32 [32768], P(('expert', 'dp')), may hold values from 0 to 63, as said below
- cotangent: bfloat16 [32768, 768], P(('expert', 'dp')), may hold values from -6 to 6
Outputs:
- output: bfloat16 [32768, 768], P(('expert', 'dp'))
- grad_inputs: bfloat16 [32768, 768], P(('expert', 'dp'))
- grad_gain_attn: float32 [768], P('dp')
- grad_w_query: float32 [768, 768], P('dp')
- grad_w_key: float32 [768, 768], P('dp')
- grad_w_value: float32 [768, 768], P('dp')
- grad_w_output: float32 [768, 768], P('dp')
- grad_bias_table: float32 [32, 12], P('dp')
- grad_gain_ffn: float32 [768], P('dp')
- grad_w_router: float32 [768, 32], P('dp')
- grad_w_in: float32 [32, 3072, 768], P('expert', 'dp')
- grad_w_out: float32 [32, 3072, 768], P('expert', 'dp')
Inputs may be any that keep to these rules, and one draw needn't show every extreme that they name: `routes`: within the 1024 tokens of one device no expert is named more than 64 times, and on every device one expert is named exactly 64 times. `slot_ids`: two tokens of one device with the same expert never share a slot. `buckets`: depends only on j - i; 0 where j = i, below 16 where j < i and 16 or more where j > i; never falls as the distance grows on either side. `segments`: never falls along a sequence.
All inputs are finite; a program needn't handle non-finite values.
Results may differ from a plain program's by a relative error of at most 0.02.
Values may be sent and summed in bfloat16 or wider, within the bound.
A program may use at most 512 MiB of HBM per device.

v0:
```python
import jax
import jax.numpy as jnp
from jax import lax
from jax.sharding import PartitionSpec as P

CAP = 64


epsilon = 1e-06


def bucket_onehot(bucket_rows, bucket_count):
    return (
        bucket_rows[:, :, None] == jnp.arange(bucket_count, dtype=jnp.int32)[None, None, :]
    ).astype(jnp.bfloat16)


def block_scores(q_rows, key_seq, bias_rows, doc_rows, doc_seq):
    raw_scores = jnp.einsum("qhd,khd->hqk", q_rows, key_seq, preferred_element_type=jnp.float32)
    same_doc = doc_rows[:, None] == doc_seq[None, :]
    return jnp.where(same_doc[None], raw_scores + bias_rows, -1000000000.0)


def norm_back(grad_norm, value, inverse, gain):
    scaled = grad_norm * gain
    grad_value = inverse * scaled - value * inverse * inverse * inverse * jnp.mean(
        scaled * value, axis=-1, keepdims=True
    )
    return (grad_value, jnp.sum(grad_norm * value * inverse, axis=0))


def on_device(
    inputs,
    gain_attn,
    w_query,
    w_key,
    w_value,
    w_output,
    bias_table,
    gain_ffn,
    w_router,
    w_in,
    w_out,
    segments,
    buckets,
    routes,
    slot_ids,
    cotangent,
):
    (
        gain_attn_all,
        query_weight,
        key_weight,
        value_weight,
        output_weight,
        table_all,
        gain_ffn_all,
        router_weight,
    ) = (
        lax.all_gather(gain_attn, "dp", axis=0, tiled=True),
        lax.all_gather(w_query, "dp", axis=0, tiled=True),
        lax.all_gather(w_key, "dp", axis=0, tiled=True),
        lax.all_gather(w_value, "dp", axis=0, tiled=True),
        lax.all_gather(w_output, "dp", axis=0, tiled=True),
        lax.all_gather(bias_table, "dp", axis=0, tiled=True),
        lax.all_gather(gain_ffn, "dp", axis=0, tiled=True),
        lax.all_gather(w_router, "dp", axis=0, tiled=True),
    )
    token_count, model_width = inputs.shape
    head_count = table_all.shape[1]
    bucket_count = table_all.shape[0]
    head_size = query_weight.shape[1] // head_count
    seq_length = buckets.shape[0]
    seq_count = token_count // seq_length
    block_rows = min(512, seq_length)
    blocks = seq_length // block_rows
    expert_count = router_weight.shape[1]

    def bias_block(block_index):
        bucket_rows = lax.dynamic_slice_in_dim(buckets, block_index * block_rows, block_rows, 0)
        return jnp.einsum(
            "qkb,bh->hqk",
            bucket_onehot(bucket_rows, bucket_count),
            table_all,
            preferred_element_type=jnp.float32,
        )

    bias_parts = lax.map(bias_block, jnp.arange(blocks, dtype=jnp.int32))
    input_float = inputs.astype(jnp.float32)
    attn_gain = gain_attn_all.astype(jnp.float32)
    inverse_attn = lax.rsqrt(jnp.mean(input_float * input_float, axis=-1, keepdims=True) + epsilon)
    normed = (input_float * inverse_attn * attn_gain).astype(jnp.bfloat16)
    query = jnp.dot(normed, query_weight, preferred_element_type=jnp.float32).astype(jnp.bfloat16)
    key_rows = jnp.dot(normed, key_weight, preferred_element_type=jnp.float32).astype(jnp.bfloat16)
    value_rows = jnp.dot(normed, value_weight, preferred_element_type=jnp.float32).astype(
        jnp.bfloat16
    )
    query_seq = query.reshape(seq_count, seq_length, head_count, head_size)
    key_seq = key_rows.reshape(seq_count, seq_length, head_count, head_size)
    value_seq = value_rows.reshape(seq_count, seq_length, head_count, head_size)

    def forward_block(block_index):
        seq_index = block_index // blocks
        inner = block_index % blocks
        row_start = inner * block_rows
        q_all = lax.dynamic_index_in_dim(query_seq, seq_index, 0, keepdims=False)
        q_rows = lax.dynamic_slice_in_dim(q_all, row_start, block_rows, 0)
        key_one = lax.dynamic_index_in_dim(key_seq, seq_index, 0, keepdims=False)
        value_one = lax.dynamic_index_in_dim(value_seq, seq_index, 0, keepdims=False)
        doc_seq = lax.dynamic_index_in_dim(segments, seq_index, 0, keepdims=False)
        doc_rows = lax.dynamic_slice_in_dim(doc_seq, row_start, block_rows, 0)
        bias_rows = lax.dynamic_index_in_dim(bias_parts, inner, 0, keepdims=False)
        scores = block_scores(q_rows, key_one, bias_rows, doc_rows, doc_seq)
        row_max = jnp.max(scores, axis=-1, keepdims=True)
        exp_scores = jnp.exp(scores - row_max)
        row_sum = jnp.sum(exp_scores, axis=-1, keepdims=True)
        attn_probs = (exp_scores / row_sum).astype(jnp.bfloat16)
        mixed = jnp.einsum(
            "hqk,khd->qhd", attn_probs, value_one, preferred_element_type=jnp.float32
        )
        return (mixed.astype(jnp.bfloat16), (row_max + jnp.log(row_sum))[:, :, 0])

    mixed_blocks, log_sums = lax.map(forward_block, jnp.arange(seq_count * blocks, dtype=jnp.int32))
    attended = mixed_blocks.reshape(token_count, head_count * head_size)
    log_sums = log_sums.reshape(seq_count, blocks, head_count, block_rows)
    branch = jnp.dot(attended, output_weight, preferred_element_type=jnp.float32)
    middle = input_float + branch
    ffn_gain = gain_ffn_all.astype(jnp.float32)
    inverse_ffn = lax.rsqrt(jnp.mean(middle * middle, axis=-1, keepdims=True) + epsilon)
    normed2 = (middle * inverse_ffn * ffn_gain).astype(jnp.bfloat16)
    logits = jnp.dot(normed2, router_weight, preferred_element_type=jnp.float32)
    router_probs = jax.nn.softmax(logits, axis=-1)
    route_pick = (routes[:, None] == jnp.arange(expert_count, dtype=jnp.int32)[None, :]).astype(
        jnp.float32
    )
    gate_value = jnp.sum(router_probs * route_pick, axis=-1)
    slot_place = routes * CAP + slot_ids
    dispatch = (
        slot_place[:, None] == jnp.arange(expert_count * CAP, dtype=jnp.int32)[None, :]
    ).astype(jnp.bfloat16)
    sent_rows = jnp.einsum(
        "ts,td->sd", dispatch, normed2, preferred_element_type=jnp.float32
    ).astype(jnp.bfloat16)
    sent_rows = sent_rows.reshape(expert_count, CAP, model_width)
    arrived = lax.all_to_all(sent_rows, "expert", split_axis=0, concat_axis=1, tiled=True)
    hidden = jnp.einsum("erd,efd->erf", arrived, w_in, preferred_element_type=jnp.float32)
    activated = jax.nn.gelu(hidden, approximate=True).astype(jnp.bfloat16)
    produced = jnp.einsum(
        "erf,efd->erd", activated, w_out, preferred_element_type=jnp.float32
    ).astype(jnp.bfloat16)
    back_rows = lax.all_to_all(produced, "expert", split_axis=1, concat_axis=0, tiled=True)
    returned = jnp.dot(
        dispatch,
        back_rows.reshape(expert_count * CAP, model_width),
        preferred_element_type=jnp.float32,
    )
    output = (middle + gate_value[:, None] * returned).astype(jnp.bfloat16)
    grad_out = cotangent.astype(jnp.float32)
    grad_gate = jnp.sum(grad_out * returned, axis=-1)
    grad_back = (gate_value[:, None] * grad_out).astype(jnp.bfloat16)
    grad_sent = jnp.einsum(
        "ts,td->sd", dispatch, grad_back, preferred_element_type=jnp.float32
    ).astype(jnp.bfloat16)
    grad_sent = grad_sent.reshape(expert_count, CAP, model_width)
    grad_produced = lax.all_to_all(grad_sent, "expert", split_axis=0, concat_axis=1, tiled=True)
    grad_act = jnp.einsum("erd,efd->erf", grad_produced, w_out, preferred_element_type=jnp.float32)
    gelu_value, gelu_pull = jax.vjp(lambda item: jax.nn.gelu(item, approximate=True), hidden)
    grad_hidden = gelu_pull(grad_act)[0].astype(jnp.bfloat16)
    grad_arrived = jnp.einsum(
        "erf,efd->erd", grad_hidden, w_in, preferred_element_type=jnp.float32
    ).astype(jnp.bfloat16)
    grad_returned = lax.all_to_all(grad_arrived, "expert", split_axis=1, concat_axis=0, tiled=True)
    grad_normed2 = jnp.dot(
        dispatch,
        grad_returned.reshape(expert_count * CAP, model_width),
        preferred_element_type=jnp.float32,
    )
    local_in = jnp.einsum("erf,erd->efd", grad_hidden, arrived, preferred_element_type=jnp.float32)
    local_out = jnp.einsum(
        "erf,erd->efd", activated, grad_produced, preferred_element_type=jnp.float32
    )
    grad_w_in, grad_w_out = (
        lax.psum_scatter(
            local_in.astype(jnp.bfloat16), "dp", scatter_dimension=1, tiled=True
        ).astype(jnp.float32),
        lax.psum_scatter(
            local_out.astype(jnp.bfloat16), "dp", scatter_dimension=1, tiled=True
        ).astype(jnp.float32),
    )
    grad_probs = route_pick * grad_gate[:, None]
    grad_logits = (
        router_probs * (grad_probs - jnp.sum(router_probs * grad_probs, axis=-1, keepdims=True))
    ).astype(jnp.bfloat16)
    router_local = jnp.einsum("td,te->de", normed2, grad_logits, preferred_element_type=jnp.float32)
    grad_normed2 = grad_normed2 + jnp.einsum(
        "te,de->td", grad_logits, router_weight, preferred_element_type=jnp.float32
    )
    grad_mid_norm, ffn_gain_local = norm_back(grad_normed2, middle, inverse_ffn, ffn_gain)
    grad_middle = grad_out + grad_mid_norm
    grad_branch = grad_middle.astype(jnp.bfloat16)
    output_local = jnp.einsum(
        "tc,td->cd", attended, grad_branch, preferred_element_type=jnp.float32
    )
    grad_attended = jnp.einsum(
        "td,cd->tc", grad_branch, output_weight, preferred_element_type=jnp.float32
    ).astype(jnp.bfloat16)
    grad_attended_seq = grad_attended.reshape(seq_count, seq_length, head_count, head_size)

    def backward_sequence(item):
        q_one, key_one, value_one, grad_one, sums_one, doc_seq = item

        def step(running, block_index):
            sum_key, sum_value, sum_table = running
            row_start = block_index * block_rows
            q_rows = lax.dynamic_slice_in_dim(q_one, row_start, block_rows, 0)
            grad_rows = lax.dynamic_slice_in_dim(grad_one, row_start, block_rows, 0)
            doc_rows = lax.dynamic_slice_in_dim(doc_seq, row_start, block_rows, 0)
            bucket_rows = lax.dynamic_slice_in_dim(buckets, row_start, block_rows, 0)
            bias_rows = lax.dynamic_index_in_dim(bias_parts, block_index, 0, keepdims=False)
            sums_rows = lax.dynamic_index_in_dim(sums_one, block_index, 0, keepdims=False)
            scores = block_scores(q_rows, key_one, bias_rows, doc_rows, doc_seq)
            attn_probs = jnp.exp(scores - sums_rows[:, :, None])
            sum_value = sum_value + jnp.einsum(
                "hqk,qhd->khd",
                attn_probs.astype(jnp.bfloat16),
                grad_rows,
                preferred_element_type=jnp.float32,
            )
            grad_weights = jnp.einsum(
                "qhd,khd->hqk", grad_rows, value_one, preferred_element_type=jnp.float32
            )
            prob_dot = jnp.sum(attn_probs * grad_weights, axis=-1, keepdims=True)
            grad_scores = (attn_probs * (grad_weights - prob_dot)).astype(jnp.bfloat16)
            grad_query = jnp.einsum(
                "hqk,khd->qhd", grad_scores, key_one, preferred_element_type=jnp.float32
            ).astype(jnp.bfloat16)
            sum_key = sum_key + jnp.einsum(
                "hqk,qhd->khd", grad_scores, q_rows, preferred_element_type=jnp.float32
            )
            sum_table = sum_table + jnp.einsum(
                "hqk,qkb->bh",
                grad_scores,
                bucket_onehot(bucket_rows, bucket_count),
                preferred_element_type=jnp.float32,
            )
            return ((sum_key, sum_value, sum_table), grad_query)

        start_state = (
            jnp.zeros((seq_length, head_count, head_size), jnp.float32),
            jnp.zeros((seq_length, head_count, head_size), jnp.float32),
            jnp.zeros((bucket_count, head_count), jnp.float32),
        )
        final_state, grad_query = lax.scan(step, start_state, jnp.arange(blocks, dtype=jnp.int32))
        return (
            grad_query.reshape(seq_length, head_count, head_size),
            final_state[0].astype(jnp.bfloat16),
            final_state[1].astype(jnp.bfloat16),
            final_state[2],
        )

    grad_q_seq, grad_k_seq, grad_v_seq, table_parts = lax.map(
        backward_sequence, (query_seq, key_seq, value_seq, grad_attended_seq, log_sums, segments)
    )
    table_local = jnp.sum(table_parts, axis=0)
    grad_q_rows = grad_q_seq.reshape(token_count, head_count * head_size)
    grad_k_rows = grad_k_seq.reshape(token_count, head_count * head_size)
    grad_v_rows = grad_v_seq.reshape(token_count, head_count * head_size)
    query_local = jnp.einsum("td,tc->dc", normed, grad_q_rows, preferred_element_type=jnp.float32)
    key_local = jnp.einsum("td,tc->dc", normed, grad_k_rows, preferred_element_type=jnp.float32)
    value_local = jnp.einsum("td,tc->dc", normed, grad_v_rows, preferred_element_type=jnp.float32)
    grad_normed = jnp.einsum(
        "tc,dc->td", grad_q_rows, query_weight, preferred_element_type=jnp.float32
    )
    grad_normed = grad_normed + jnp.einsum(
        "tc,dc->td", grad_k_rows, key_weight, preferred_element_type=jnp.float32
    )
    grad_normed = grad_normed + jnp.einsum(
        "tc,dc->td", grad_v_rows, value_weight, preferred_element_type=jnp.float32
    )
    grad_in_norm, attn_gain_local = norm_back(grad_normed, input_float, inverse_attn, attn_gain)
    grad_inputs = (grad_middle + grad_in_norm).astype(jnp.bfloat16)
    (
        total_gain_a,
        total_query,
        total_key,
        total_value,
        total_output,
        total_table,
        total_gain_f,
        total_router,
    ) = (
        lax.psum(attn_gain_local.astype(jnp.bfloat16), "expert").astype(jnp.float32),
        lax.psum(query_local.astype(jnp.bfloat16), "expert").astype(jnp.float32),
        lax.psum(key_local.astype(jnp.bfloat16), "expert").astype(jnp.float32),
        lax.psum(value_local.astype(jnp.bfloat16), "expert").astype(jnp.float32),
        lax.psum(output_local.astype(jnp.bfloat16), "expert").astype(jnp.float32),
        lax.psum(table_local.astype(jnp.bfloat16), "expert").astype(jnp.float32),
        lax.psum(ffn_gain_local.astype(jnp.bfloat16), "expert").astype(jnp.float32),
        lax.psum(router_local.astype(jnp.bfloat16), "expert").astype(jnp.float32),
    )
    (
        grad_gain_attn,
        grad_w_query,
        grad_w_key,
        grad_w_value,
        grad_w_output,
        grad_bias_table,
        grad_gain_ffn,
        grad_w_router,
    ) = (
        lax.psum_scatter(
            total_gain_a.astype(jnp.bfloat16), "dp", scatter_dimension=0, tiled=True
        ).astype(jnp.float32),
        lax.psum_scatter(
            total_query.astype(jnp.bfloat16), "dp", scatter_dimension=0, tiled=True
        ).astype(jnp.float32),
        lax.psum_scatter(
            total_key.astype(jnp.bfloat16), "dp", scatter_dimension=0, tiled=True
        ).astype(jnp.float32),
        lax.psum_scatter(
            total_value.astype(jnp.bfloat16), "dp", scatter_dimension=0, tiled=True
        ).astype(jnp.float32),
        lax.psum_scatter(
            total_output.astype(jnp.bfloat16), "dp", scatter_dimension=0, tiled=True
        ).astype(jnp.float32),
        lax.psum_scatter(
            total_table.astype(jnp.bfloat16), "dp", scatter_dimension=0, tiled=True
        ).astype(jnp.float32),
        lax.psum_scatter(
            total_gain_f.astype(jnp.bfloat16), "dp", scatter_dimension=0, tiled=True
        ).astype(jnp.float32),
        lax.psum_scatter(
            total_router.astype(jnp.bfloat16), "dp", scatter_dimension=0, tiled=True
        ).astype(jnp.float32),
    )
    return (
        output,
        grad_inputs,
        grad_gain_attn,
        grad_w_query,
        grad_w_key,
        grad_w_value,
        grad_w_output,
        grad_bias_table,
        grad_gain_ffn,
        grad_w_router,
        grad_w_in,
        grad_w_out,
    )


def solution(mesh):
    placed = (
        P(("expert", "dp"), None),
        P("dp"),
        P("dp", None),
        P("dp", None),
        P("dp", None),
        P("dp", None),
        P("dp", None),
        P("dp"),
        P("dp", None),
        P("expert", None, None),
        P("expert", None, None),
        P(("expert", "dp"), None),
        P(),
        P(("expert", "dp")),
        P(("expert", "dp")),
        P(("expert", "dp"), None),
    )
    return jax.shard_map(
        on_device,
        mesh=mesh,
        in_specs=placed,
        out_specs=(
            P(("expert", "dp"), None),
            P(("expert", "dp"), None),
            P("dp"),
            P("dp", None),
            P("dp", None),
            P("dp", None),
            P("dp", None),
            P("dp", None),
            P("dp"),
            P("dp", None),
            P("expert", "dp", None),
            P("expert", "dp", None),
        ),
        check_vma=False,
    )
```

profile of v0, /device:TPU:0, one launch (start us, length us, event | category | flops | bytes accessed | tf_op | source)
XLA Modules:
  0.0 1755.5 jit_solution(3694644486916548352)
XLA Ops:
  14.0 18.2 %all-reduce.6 = (bf16[768]{0:T(1024)(128)(2,1)S(1)}, bf16[768]{0:T(1024)(128)(2,1)S(1)}) all-reduce(bf16[768]{0:T(1024)(128)(2,1)S(1)} %dynamic-update-slice, bf16[768]{0:T(1024)(128)(2,1)S(1)} %dynamic-update-slice.1), channel_id=1, replica_groups=mesh['expert'=4,'dp'=8] {'dp'}, use_global_device_ids=true, to_apply=%add | all-reduce | flops 1536 | bytes 6144
  40.7 91.0 %while.54 = (s32[]{:T(128)}, f32[2,12,512,1024]{3,2,1,0:T(8,128)}, s32[2]{0:T(128)S(1)}, s32[1024,1024]{1,0:T(8,128)}, bf16[32,12]{0,1:T(8,128)(2,1)S(1)}, /*index=5*/s32[]{:T(128)}, s32[1]{0:T(128)}, s32[]{:T(128)}, s32[]{:T(128)}) while((s32[]{:T(128)}, f32[2,12,512,1024]{3,2,1,0:T(8,128)}, s32[2]{0:T(128)S(1)}, s32[1024,1024]{1,0:T(8,128)}, ...), condition=%wide.region_2.3_spmd, body=%wide.region_1.2_spmd.sunk | while | flops 419430400 | bytes 90178968 | solution.py:88
  43.8 16.1 fusion.165
  59.8 26.4 %copy_dynamic-update-slice_fusion.2 = f32[2,12,512,1024]{3,2,1,0:T(8,128)} fusion(f32[2,12,512,1024]{3,2,1,0:T(8,128)} %get-tuple-element.800, s32[]{:T(128)} %get-tuple-element.799, f32[1,12,512,1024]{3,1,2,0:T(8,128)} %fusion.165), kind=kLoop, calls=%fused_computation.3.clone.1 | loop fusion | bytes 58720768 | tf_op jit(solution)/shard_map/while/body/jit(dynamic_update_index_in_dim)/dynamic_update_slice | solution.py:88
  89.2 16.1 fusion.165
  105.3 26.3 %copy_dynamic-update-slice_fusion.2 = f32[2,12,512,1024]{3,2,1,0:T(8,128)} fusion(f32[2,12,512,1024]{3,2,1,0:T(8,128)} %get-tuple-element.800, s32[]{:T(128)} %get-tuple-element.799, f32[1,12,512,1024]{3,1,2,0:T(8,128)} %fusion.165), kind=kLoop, calls=%fused_computation.3.clone.1 | loop fusion | bytes 58720768 | tf_op jit(solution)/shard_map/while/body/jit(dynamic_update_index_in_dim)/dynamic_update_slice | solution.py:88
  144.3 84.1 %while.55 = (s32[]{:T(128)}, bf16[2,512,12,64]{1,3,2,0:T(8,128)(2,1)}, f32[2,12,512]{2,1,0:T(8,128)S(1)}, s32[2]{0:T(128)S(1)}, s32[1,1024]{1,0:T(1,128)S(1)}, /...) while((s32[]{:T(128)}, ...), condition=%wide.region_6.7_spmd, body=%wide.region_3.6_spmd.sunk | while | flops 1661855744 | bytes 106662744 | solution.py:123
  189.9 16.2 fusion.167
  243.1 41.0 %all_to_all.66 = bf16[32,64,768]{2,1,0:T(8,128)(2,1)S(1)} all-to-all(bf16[32,64,768]{2,1,0:T(8,128)(2,1)S(1)} %bitcast.219), channel_id=1, replica_groups=mesh['expert'=4,'dp'=8] {'expert'}, dimensions={0} | all-to-all | bytes 6291456 | tf_op jit(solution)/shard_map/all_to_all | solution.py:145
  284.4 23.7 %fusion.103 = f32[8,256,3072]{2,1,0:T(8,128)} fusion(bf16[8,256,768]{2,1,0:T(8,128)(2,1)S(1)} %bitcast.205, bf16[8,3072,768]{2,1,0:T(8,128)(2,1)} %param.31), kind=kOutput, calls=%fused_computation.140 | convolution fusion | flops 9663676416 | bytes 66060288 | tf_op jit(solution)/shard_map/erd,efd->erf/dot_general | solution.py:146
  308.1 28.0 %convolution_convert_fusion.4 = bf16[8,256,768]{2,1,0:T(8,128)(2,1)} fusion(bf16[8,3072,768]{2,1,0:T(8,128)(2,1)} %param.32, f32[8,256,3072]{2,1,0:T(8,128)} %fusion.103), kind=kOutput, calls=%fused_computation.107 | convolution fusion | flops 9721872384 | bytes 66060288 | tf_op jit(solution)/shard_map/erf,efd->erd/dot_general | solution.py:148
  364.0 16.6 all-to-all-done.1
  391.7 38.8 %all_to_all.67 = bf16[32,64,768]{2,1,0:T(8,128)(2,1)S(1)} all-to-all(bf16[32,64,768]{2,1,0:T(8,128)(2,1)S(1)} %bitcast.220), channel_id=1, replica_groups=mesh['expert'=4,'dp'=8] {'expert'}, dimensions={0} | all-to-all | bytes 6291456 | tf_op jit(solution)/shard_map/all_to_all | solution.py:165
  430.7 31.7 %fusion.49 = bf16[8,256,3072]{2,1,0:T(8,128)(2,1)} fusion(f32[8,256,3072]{2,1,0:T(8,128)} %fusion.103, bf16[8,256,768]{2,1,0:T(8,128)(2,1)S(1)} %bitcast.215, bf16[8,3072,768]{2,1,0:T(8,128)(2,1)} %param.32), kind=kOutput, calls=%fused_computation.62 | convolution fusion | flops 9789505536 | bytes 78643200 | tf_op jit(solution)/shard_map/erd,efd->erf/dot_general | solution.py:166
  462.3 21.5 %convolution_convert_fusion.3 = bf16[8,256,768]{2,1,0:T(8,128)(2,1)} fusion(bf16[8,256,3072]{2,1,0:T(8,128)(2,1)} %fusion.49, bf16[8,3072,768]{2,1,0:T(8,128)(2,1)} %param.31), kind=kOutput, calls=%fused_computation.106 | convolution fusion | flops 9665249280 | bytes 53477376 | tf_op jit(solution)/shard_map/erf,efd->erd/dot_general | solution.py:169
  493.3 33.6 %all-to-all-done.3 = bf16[8,256,768]{2,0,1:T(8,128)(2,1)S(1)} async-done(((bf16[8,256,768]{2,0,1:T(8,128)(2,1)}), bf16[8,256,768]{2,0,1:T(8,128)(2,1)S(1)}, u32[]{:S(2)}, u32[]{:S(2)}) %all-to-all-start.3) | async-done | bytes 3145760 | tf_op jit(solution)/shard_map/all_to_all | solution.py:172
  547.5 275.8 %while.56 = (s32[]{:T(128)}, f32[1024,12,64]{0,2,1:T(8,128)}, f32[1024,12,64]{0,2,1:T(8,128)}, f32[32,12]{0,1:T(8,128)S(1)}, bf16[2,512,12,64]{1,3,2,0:T(8,128)(...) while((s32[]{:T(128)}, f32[1024,12,64]{0,2,1:T(8,128)}, ...), condition=%wide.region_16.17_spmd.clone, body=%wide.region_14.16_spmd.clone.sunk | while | flops 4506643456 | bytes 290854720 | solution.py:253
  563.5 26.8 %multiply_reduce_fusion.5 = (f32[12,512]{1,0:T(8,128)S(1)}, f32[12,512,1024]{2,1,0:T(8,128)}) fusion(f32[12,512,1024]{2,1,0:T(8,128)} %fusion.180, f32[12,512]{1,0:T(8,128)S(1)} %dynamic-slice_bitcast_fusion.2, f32[2,12,512,1024]{3,2,1,0:T(8,128)} %get-tuple-element.906, s32[]{:T(128)S(6)} %select_n.78, ...), kind=kOutput, calls=%fused_computation.32.clone.1 | convolution fusion | flops 836757504 | bytes 78430216 | tf_op jit(solution)/shard_map/while/body/eval_jaxpr/while/body/eval_jaxpr/qhd,khd->hqk/dot_general | solution.py:19
  590.4 21.1 %multiply_convert_fusion.6 = bf16[12,512,1024]{2,1,0:T(8,128)(2,1)} fusion(f32[12,512,1024]{2,1,0:T(8,128)} %get-tuple-element.788, f32[12,512,1024]{2,1,0:T(8,128)} %fusion.180, f32[12,512]{1,0:T(8,128)S(1)} %get-tuple-element.789), kind=kLoop, calls=%fused_computation.31.clone.1 | loop fusion | flops 18874368 | bytes 62939136 | tf_op jit(solution)/shard_map/while/body/eval_jaxpr/while/body/eval_jaxpr/convert_element_type | solution.py:233
  611.5 22.9 %copy.182 = bf16[12,512,1024]{1,0,2:T(8,128)(2,1)} copy(bf16[12,512,1024]{2,1,0:T(8,128)(2,1)} %multiply_convert_fusion.6) | data formatting | bytes 25165824 | tf_op jit(solution)/shard_map/while/body/eval_jaxpr/while/body/eval_jaxpr/convert_element_type | solution.py:233
  700.5 26.5 %multiply_reduce_fusion.5 = (f32[12,512]{1,0:T(8,128)S(1)}, f32[12,512,1024]{2,1,0:T(8,128)}) fusion(f32[12,512,1024]{2,1,0:T(8,128)} %fusion.180, f32[12,512]{1,0:T(8,128)S(1)} %dynamic-slice_bitcast_fusion.2, f32[2,12,512,1024]{3,2,1,0:T(8,128)} %get-tuple-element.906, s32[]{:T(128)S(6)} %select_n.78, ...), kind=kOutput, calls=%fused_computation.32.clone.1 | convolution fusion | flops 836757504 | bytes 78430216 | tf_op jit(solution)/shard_map/while/body/eval_jaxpr/while/body/eval_jaxpr/qhd,khd->hqk/dot_general | solution.py:19
  726.9 21.1 %multiply_convert_fusion.6 = bf16[12,512,1024]{2,1,0:T(8,128)(2,1)} fusion(f32[12,512,1024]{2,1,0:T(8,128)} %get-tuple-element.788, f32[12,512,1024]{2,1,0:T(8,128)} %fusion.180, f32[12,512]{1,0:T(8,128)S(1)} %get-tuple-element.789), kind=kLoop, calls=%fused_computation.31.clone.1 | loop fusion | flops 18874368 | bytes 62939136 | tf_op jit(solution)/shard_map/while/body/eval_jaxpr/while/body/eval_jaxpr/convert_element_type | solution.py:233
  748.1 22.9 %copy.182 = bf16[12,512,1024]{1,0,2:T(8,128)(2,1)} copy(bf16[12,512,1024]{2,1,0:T(8,128)(2,1)} %multiply_convert_fusion.6) | data formatting | bytes 25165824 | tf_op jit(solution)/shard_map/while/body/eval_jaxpr/while/body/eval_jaxpr/convert_element_type | solution.py:233
  844.2 17.9 %reduce-scatter.14.cloned.1.call-done = bf16[96,768]{1,0:T(8,128)(2,1)} async-done(((bf16[768,768]{1,0:T(8,128)(2,1)}), bf16[96,768]{1,0:T(8,128)(2,1)}) %reduce-scatter.14.cloned.1.call-update) | async-done | bytes 147472 | tf_op jit(solution)/shard_map/reduce_scatter | solution.py:314
  862.1 33.3 %reduce-scatter.16.cloned.1.call-done = bf16[96,768]{1,0:T(8,128)(2,1)} async-done(((bf16[768,768]{1,0:T(8,128)(2,1)}), bf16[96,768]{1,0:T(8,128)(2,1)}) %reduce-scatter.16.cloned.1.call-update) | async-done | bytes 147472 | tf_op jit(solution)/shard_map/reduce_scatter | solution.py:317
  895.4 33.3 %reduce-scatter.18.cloned.1.call-done = bf16[96,768]{1,0:T(8,128)(2,1)} async-done(((bf16[768,768]{1,0:T(8,128)(2,1)}), bf16[96,768]{1,0:T(8,128)(2,1)}) %reduce-scatter.18.cloned.1.call-update) | async-done | bytes 147472 | tf_op jit(solution)/shard_map/reduce_scatter | solution.py:320
  928.8 25.1 %convolution_convert_fusion.1 = bf16[8,3072,768]{2,1,0:T(8,128)(2,1)} fusion(bf16[8,256,768]{2,1,0:T(8,128)(2,1)} %bitcast.216, f32[8,256,3072]{2,1,0:T(8,128)} %fusion.103), kind=kOutput, calls=%fused_computation.64 | convolution fusion | flops 9739173888 | bytes 66060288 | tf_op jit(solution)/shard_map/erf,erd->efd/dot_general | solution.py:179
  955.8 25.5 %convolution_convert_fusion.2 = bf16[8,3072,768]{2,1,0:T(8,128)(2,1)} fusion(bf16[8,256,3072]{2,1,0:T(8,128)(2,1)} %fusion.49, bf16[8,256,768]{2,1,0:T(8,128)(2,1)S(1)} %bitcast.206), kind=kOutput, calls=%fused_computation.65 | convolution fusion | flops 9682550784 | bytes 53477376 | tf_op jit(solution)/shard_map/erf,erd->efd/dot_general | solution.py:178
  991.5 26.1 %all-reduce.5 = (bf16[768]{0:T(1024)(128)(2,1)S(1)}, bf16[32,12]{1,0:T(8,128)(2,1)S(1)}, bf16[768]{0:T(1024)(128)(2,1)S(1)}) all-reduce(bf16[768]{0:T(1024)(128)(2,1)S(1)} %get-tuple-element.522, bf16[32,12]{1,0:T(8,128)(2,1)S(1)} %copy.146, bf16[768]{0:T(1024)(128)(2,1)S(1)} %copy-done.56), channel_id=2, replica_groups=mesh['expert'=4,'dp'=8] {'dp'}, use_global_device_ids=true, to_apply=%region_20.21.clone | all-reduce | flops 1920 | bytes 7680
  1017.7 16.3 all-reduce.7
  1050.0 325.6 %reduce-scatter.12.cloned.1.call-done = bf16[8,384,768]{2,1,0:T(8,128)(2,1)} async-done(((bf16[8,3072,768]{2,1,0:T(8,128)(2,1)}), bf16[8,384,768]{2,1,0:T(8,128)(2,1)}) %reduce-scatter.12.cloned.1.call-update) | async-done | bytes 4718608 | tf_op jit(solution)/shard_map/reduce_scatter | solution.py:186
  1382.5 358.7 %reduce-scatter.10.cloned.1.call-done = bf16[8,384,768]{2,1,0:T(8,128)(2,1)} async-done(((bf16[8,3072,768]{2,1,0:T(8,128)(2,1)}), bf16[8,384,768]{2,1,0:T(8,128)(2,1)}) %reduce-scatter.10.cloned.1.call-update) | async-done | bytes 4718608 | tf_op jit(solution)/shard_map/reduce_scatter | solution.py:183
  (289 shorter events, 369.0 us)
Async XLA Ops:
  7.2 6.5 copy-start.64
  7.2 25.0 %copy-start.60 = (bf16[4,12]{1,0:T(4,128)(2,1)S(1)}, bf16[4,12]{1,0:T(4,128)(2,1)}, u32[]{:S(2)}) copy-start(bf16[4,12]{1,0:T(4,128)(2,1)} %param.28) | copy-start | bytes 292
  7.2 125.7 %all-gather.7.cloned.1.call-start = ((), (), s32[]{:S(2)}) async-start(), calls=%async_computation.11 | async-start | bytes 1327104 | tf_op jit(solution)/shard_map/all_gather | solution.py:61
  8.0 128.9 %all-gather.9.cloned.1.call-start = ((), (), s32[]{:S(2)}) async-start(), calls=%async_computation.12 | async-start | bytes 1327104 | tf_op jit(solution)/shard_map/all_gather | solution.py:62
  8.7 131.0 %all-gather.11.cloned.1.call-start = ((), (), s32[]{:S(2)}) async-start(), calls=%async_computation.13 | async-start | bytes 1327104 | tf_op jit(solution)/shard_map/all_gather | solution.py:63
  9.4 224.9 %all-gather.13.cloned.1.call-start = ((), (), s32[]{:S(2)}) async-start(), calls=%async_computation.14 | async-start | bytes 1327104 | tf_op jit(solution)/shard_map/all_gather | solution.py:64
  11.8 125.1 %copy-start.10 = (bf16[1024,768]{0,1:T(8,128)(2,1)}, bf16[1024,768]{0,1:T(8,128)(2,1)S(1)}, u32[]{:S(2)}) copy-start(bf16[1024,768]{0,1:T(8,128)(2,1)S(1)} %copy.124) | copy-start | bytes 4718596
  12.2 127.6 %copy-start.42 = (f32[1024]{0:T(1024)}, f32[1024]{0:T(1024)S(1)}, u32[]{:S(2)}) copy-start(f32[1024]{0:T(1024)S(1)} %add_rsqrt_fusion.1) | copy-start | bytes 12292
  32.2 107.5 %copy-start.44 = (f32[768]{0:T(1024)}, f32[768]{0:T(1024)S(1)}, u32[]{:S(2)}) copy-start(f32[768]{0:T(1024)S(1)} %convert_element_type.179) | copy-start | bytes 9220
  40.7 91.6 %copy-start.46 = (s32[1024]{0:T(1024)S(1)}, s32[1024]{0:T(1024)}, u32[]{:S(2)}) copy-start(s32[1024]{0:T(1024)} %param.35) | copy-start | bytes 12292
  40.7 91.6 %copy-start.57 = (s32[1024]{0:T(1024)S(1)}, s32[1024]{0:T(1024)}, u32[]{:S(2)}) copy-start(s32[1024]{0:T(1024)} %param.36) | copy-start | bytes 12292
  284.4 23.7 %copy-start.6 = (bf16[4,8,64,768]{3,2,0,1:T(8,128)(2,1)}, bf16[4,8,64,768]{3,2,0,1:T(8,128)(2,1)S(1)}, u32[]{:S(2)}) copy-start(bf16[4,8,64,768]{3,2,0,1:T(8,128)(2,1)S(1)} %copy.129) | copy-start | bytes 9437188
  341.4 39.2 %all-to-all-start.1 = ((bf16[8,256,768]{2,0,1:T(8,128)(2,1)}), bf16[8,256,768]{2,0,1:T(8,128)(2,1)S(1)}, u32[]{:S(2)}, u32[]{:S(2)}) async-start(bf16[8,256,768]{2,0,1:T(8,128)(2,1)} %copy.130), calls=%async_computation.1 | async-start | bytes 6291456 | tf_op jit(solution)/shard_map/all_to_all | solution.py:151
  363.9 167.7 %copy-start.24 = (f32[1024,32]{0,1:T(8,128)}, f32[1024,32]{0,1:T(8,128)S(1)}, u32[]{:S(2)}) copy-start(f32[1024,32]{0,1:T(8,128)S(1)} %get-tuple-element.608) | copy-start | bytes 393220
  363.9 167.7 %copy-start.40 = (f32[1024]{0:T(1024)}, f32[1024]{0:T(1024)S(1)}, u32[]{:S(2)}) copy-start(f32[1024]{0:T(1024)S(1)} %get-tuple-element.607) | copy-start | bytes 12292
  364.0 167.6 %copy-start.49 = (f32[1024]{0:T(1024)}, f32[1024]{0:T(1024)S(1)}, u32[]{:S(2)}) copy-start(f32[1024]{0:T(1024)S(1)} %fusion.89) | copy-start | bytes 12292
  387.4 144.2 %copy-start.51 = (f32[1024]{0:T(1024)}, f32[1024]{0:T(1024)S(1)}, u32[]{:S(2)}) copy-start(f32[1024]{0:T(1024)S(1)} %get-tuple-element.605) | copy-start | bytes 12292
  387.5 144.1 %copy-start.53 = (f32[1024]{0:T(1024)}, f32[1024]{0:T(1024)S(1)}, u32[]{:S(2)}) copy-start(f32[1024]{0:T(1024)S(1)} %get-tuple-element.524) | copy-start | bytes 12292
  430.6 31.7 %copy-start.22 = (bf16[4,8,64,768]{3,2,0,1:T(8,128)(2,1)}, bf16[4,8,64,768]{3,2,0,1:T(8,128)(2,1)S(1)}, u32[]{:S(2)}) copy-start(bf16[4,8,64,768]{3,2,0,1:T(8,128)(2,1)S(1)} %copy.134) | copy-start | bytes 9437188
  489.1 37.8 %all-to-all-start.3 = ((bf16[8,256,768]{2,0,1:T(8,128)(2,1)}), bf16[8,256,768]{2,0,1:T(8,128)(2,1)S(1)}, u32[]{:S(2)}, u32[]{:S(2)}) async-start(bf16[8,256,768]{2,0,1:T(8,128)(2,1)} %copy.135), calls=%async_computation.3 | async-start | bytes 6291456 | tf_op jit(solution)/shard_map/all_to_all | solution.py:172
  492.8 351.4 %reduce-scatter.20.cloned.1.call-start = ((), (), s32[]{:S(2)}) async-start(), calls=%async_computation.20 | async-start | bytes 1327104 | tf_op jit(solution)/shard_map/reduce_scatter | solution.py:323
  541.2 6.4 copy-start.1
  541.2 6.4 copy-start.3
  541.2 320.9 %reduce-scatter.14.cloned.1.call-start = ((), (), s32[]{:S(2)}) async-start(), calls=%async_computation.17 | async-start | bytes 1327104 | tf_op jit(solution)/shard_map/reduce_scatter | solution.py:314
  640.5 13.8 copy-start.5
  777.1 13.8 copy-start.5
  830.6 64.8 %reduce-scatter.16.cloned.1.call-start = ((), (), s32[]{:S(2)}) async-start(), calls=%async_computation.18 | async-start | bytes 1327104 | tf_op jit(solution)/shard_map/reduce_scatter | solution.py:317
  838.0 90.6 %reduce-scatter.18.cloned.1.call-start = ((), (), s32[]{:S(2)}) async-start(), calls=%async_computation.19 | async-start | bytes 1327104 | tf_op jit(solution)/shard_map/reduce_scatter | solution.py:320
  842.6 140.2 %reduce-scatter.22.cloned.1.call-start = ((), (), s32[]{:S(2)}) async-start(), calls=%async_computation.21 | async-start | bytes 221184
  844.2 199.3 %all-reduce.11.cloned.1.call-start = ((), (), s32[]{:S(2)}) async-start(), calls=%async_computation.22 | async-start | bytes 1179648 | tf_op jit(solution)/shard_map/psum | solution.py:293
  928.7 446.9 %reduce-scatter.12.cloned.1.call-start = ((), (), s32[]{:S(2)}) async-start(), calls=%async_computation.16 | async-start | bytes 42467328 | tf_op jit(solution)/shard_map/reduce_scatter | solution.py:186
  953.9 787.4 %reduce-scatter.10.cloned.1.call-start = ((), (), s32[]{:S(2)}) async-start(), calls=%async_computation.15 | async-start | bytes 42467328 | tf_op jit(solution)/shard_map/reduce_scatter | solution.py:183
  (48 other events, 161.3 us)
Sparse Core Ops, SparseCore 0:
  9.7 25.5 all-gather.6
  36.9 22.2 all-gather.8
  60.9 22.4 all-gather.10
  84.8 22.4 all-gather.12
  541.3 31.4 reduce-scatter.19
  830.7 31.3 reduce-scatter.13
  864.4 30.9 reduce-scatter.15
  897.7 30.9 reduce-scatter.17
  931.5 28.6 reduce-scatter.21
  963.5 44.6 all-reduce.10
  1010.6 364.9 reduce-scatter.11
  1378.0 363.2 reduce-scatter.9
where the time goes:
time: 1770 us; the launch traced here: 1760 us
  waiting for transfers between devices  822 us (46%)
  matrix products  467 us (26%)
  local copies, waits for them, and re-layouts  164 us (9%)
  blocking collectives  163 us (9%)
  other arithmetic  103 us (6%)
  between operations  17.7 us (1%)
    reduce_scatter x1, waiting for transfers between devices, on_device(): lax.psum_scatter(local_in.astype(jnp.bfloat16), 'dp', scatter_dimension=1...  359 us
    reduce_scatter x1, waiting for transfers between devices, on_device(): lax.psum_scatter(local_out.astype(jnp.bfloat16), 'dp', scatter_dimension=...  326 us
    dot_general x4, matrix products, block_scores(): jnp.einsum('qhd,khd->hqk', q_rows, key_seq, preferred_element_type=jnp.fl...  85.5 us
    dynamic_update_slice x2, local copies, waits for them, and re-layouts, on_device(): bias_parts = lax.map(bias_block, jnp.arange(blocks, dtype=jnp.int32))  52.7 us
    convert_element_type x2, local copies, waits for them, and re-layouts, step(): grad_scores = (attn_probs * (grad_weights - prob_dot)).astype(jnp.bfloat16)  45.9 us
    unnamed x2, blocking collectives  44.3 us
    convert_element_type x2, other arithmetic, step(): grad_scores = (attn_probs * (grad_weights - prob_dot)).astype(jnp.bfloat16)  42.3 us
    all_to_all x1, blocking collectives, on_device(): lax.all_to_all(sent_rows, 'expert', split_axis=0, concat_axis=1, tiled=True)  41 us
  transfers between devices with their start and end apart: 14, of which 7 were waited for; matrix products, arithmetic and copies ran while one was open for 32% of the time, Pallas kernels for 0%

commit v1 on v0

v1 whole, which is shorter than its diff:
```python
import functools

import jax
import jax.numpy as jnp
from jax import lax
from jax.experimental import pallas as pl
from jax.experimental.pallas import tpu as pltpu
from jax.sharding import PartitionSpec as P

CAP = 64


epsilon = 1e-06


def diagonal_buckets(buckets):
    length = buckets.shape[0]
    return jnp.concatenate([buckets[length - 1, : length - 1], buckets[0], buckets[0, -1:]])


LANES = 128


def bias_strip(diagonal):
    wide = jnp.broadcast_to(diagonal, (LANES, diagonal.shape[1]))
    return pltpu.roll(wide, wide.shape[1] - (LANES - 1), 1, stride=1, stride_axis=0)


def head_scores(q, key, strip, first, docs_rows, docs_seq):
    length = key.shape[0]
    tiles = []
    for row in range(first, first + q.shape[0], LANES):
        start = length - LANES - row
        tiles.append(strip[:, start : start + length])
    raw = dot_nt(q, key) + jnp.concatenate(tiles, axis=0)
    return jnp.where(docs_rows == docs_seq, raw, -1000000000.0)


def attend_kernel(size, rows, q_ref, k_ref, v_ref, diag_ref, col_ref, row_ref, out_ref, lse_ref):
    length = q_ref.shape[0]
    docs_seq = row_ref[0]
    for head in range(q_ref.shape[1] // size):
        own = slice(head * size, (head + 1) * size)
        key, value = k_ref[:, own], v_ref[:, own]
        strip = bias_strip(diag_ref[0, head : head + 1, :])
        for first in range(0, length, rows):
            part = slice(first, first + rows)
            scores = head_scores(q_ref[part, own], key, strip, first, col_ref[0, part, :], docs_seq)
            top = jnp.max(scores, axis=-1, keepdims=True)
            weights = jnp.exp(scores - top)
            total = jnp.sum(weights, axis=-1, keepdims=True)
            probs = (weights * (1.0 / total)).astype(jnp.bfloat16)
            out_ref[part, own] = dot_nn(probs, value).astype(jnp.bfloat16)
            lse_ref[0, 0, part, head : head + 1] = top + jnp.log(total)


def attend_back_kernel(
    size,
    rows,
    q_ref,
    k_ref,
    v_ref,
    grad_ref,
    diag_ref,
    col_ref,
    row_ref,
    lse_ref,
    gq_ref,
    gk_ref,
    gv_ref,
    gd_ref,
    sum_k,
    sum_v,
    sum_s,
):
    length = q_ref.shape[0]
    docs_seq = row_ref[0]
    sum_k[...] = jnp.zeros_like(sum_k)
    sum_v[...] = jnp.zeros_like(sum_v)
    for head in range(q_ref.shape[1] // size):
        own = slice(head * size, (head + 1) * size)
        key, value = k_ref[:, own], v_ref[:, own]
        strip = bias_strip(diag_ref[0, head : head + 1, :])
        sum_s[...] = jnp.zeros_like(sum_s)
        for first in range(0, length, rows):
            part = slice(first, first + rows)
            q, grad = q_ref[part, own], grad_ref[part, own]
            scores = head_scores(q, key, strip, first, col_ref[0, part, :], docs_seq)
            probs = jnp.exp(scores - lse_ref[0, 0, part, head : head + 1])
            sum_v[own, :] += dot_nn(grad.T, probs.astype(jnp.bfloat16))
            grad_probs = dot_nt(grad, value)
            mean = jnp.sum(probs * grad_probs, axis=-1, keepdims=True)
            grad_scores = (probs * (grad_probs - mean)).astype(jnp.bfloat16)
            gq_ref[part, own] = dot_nn(grad_scores, key).astype(jnp.bfloat16)
            sum_k[own, :] += dot_nn(q.T, grad_scores)
            for row in range(0, rows, LANES):
                start = length - LANES - first - row
                sum_s[:, start : start + length] += grad_scores[row : row + LANES].astype(
                    jnp.float32
                )
        folded = sum_s[...]
        width = folded.shape[1]
        half = LANES // 2
        while half >= 1:
            folded = folded[:half] + pltpu.roll(folded[half:], width - half, 1)
            half = half // 2
        gd_ref[0, 0, head : head + 1, :] = pltpu.roll(folded, LANES - 1, 1)
    gk_ref[...] = sum_k[...].T.astype(jnp.bfloat16)
    gv_ref[...] = sum_v[...].T.astype(jnp.bfloat16)


def attention_specs(tokens, length, width, size, whole):
    pack = LANES // size
    packs = width // LANES
    column = lambda k: pl.BlockSpec((length, LANES), lambda s, h: (s, h + k * packs))
    return dict(
        grid=(tokens // length, packs),
        qkv=[column(0), column(1), column(2)],
        rows=column(0),
        diag=pl.BlockSpec((1, pack, whole), lambda s, h: (h, 0, 0)),
        col=pl.BlockSpec((1, length, 1), lambda s, h: (s, 0, 0)),
        row=pl.BlockSpec((1, 1, length), lambda s, h: (s, 0, 0)),
        lse=pl.BlockSpec((1, 1, length, pack), lambda s, h: (s, h, 0, 0)),
    )


def attend(qkv, diagonals, segments, size):
    tokens, width = qkv.shape[0], qkv.shape[1] // 3
    seqs, length = segments.shape
    pack, packs = LANES // size, width // LANES
    whole = diagonals.shape[1]
    specs = attention_specs(tokens, length, width, size, whole)
    pairs = tokens * length * width
    return pl.pallas_call(
        functools.partial(attend_kernel, size, 256),
        grid=specs["grid"],
        in_specs=specs["qkv"] + [specs["diag"], specs["col"], specs["row"]],
        out_specs=[specs["rows"], specs["lse"]],
        out_shape=[
            jax.ShapeDtypeStruct((tokens, width), jnp.bfloat16),
            jax.ShapeDtypeStruct((seqs, packs, length, pack), jnp.float32),
        ],
        compiler_params=pltpu.CompilerParams(vmem_limit_bytes=56 * 2**20),
        cost_estimate=pl.CostEstimate(
            flops=16 * pairs, bytes_accessed=10 * qkv.size, transcendentals=pairs // size
        ),
        name="attend",
    )(
        qkv,
        qkv,
        qkv,
        diagonals.reshape(packs, pack, whole),
        segments[:, :, None],
        segments[:, None, :],
    )


def attend_back(qkv, grad, diagonals, segments, lse, size):
    tokens, width = grad.shape
    seqs, length = segments.shape
    pack, packs = LANES // size, width // LANES
    whole = diagonals.shape[1]
    specs = attention_specs(tokens, length, width, size, whole)
    pairs = tokens * length * width
    rows_shape = jax.ShapeDtypeStruct((tokens, width), jnp.bfloat16)
    gq, gk, gv, gd = pl.pallas_call(
        functools.partial(attend_back_kernel, size, 256),
        grid=specs["grid"],
        in_specs=specs["qkv"]
        + [specs["rows"], specs["diag"], specs["col"], specs["row"], specs["lse"]],
        out_specs=[specs["rows"]] * 3
        + [pl.BlockSpec((1, 1, pack, whole), lambda s, h: (s, h, 0, 0))],
        out_shape=[rows_shape] * 3 + [jax.ShapeDtypeStruct((seqs, packs, pack, whole), jnp.float32)],
        scratch_shapes=[
            pltpu.VMEM((LANES, length), jnp.float32),
            pltpu.VMEM((LANES, length), jnp.float32),
            pltpu.VMEM((LANES, whole), jnp.float32),
        ],
        compiler_params=pltpu.CompilerParams(vmem_limit_bytes=56 * 2**20),
        cost_estimate=pl.CostEstimate(
            flops=40 * pairs, bytes_accessed=16 * qkv.size, transcendentals=pairs // size
        ),
        name="attend_back",
    )(
        qkv,
        qkv,
        qkv,
        grad,
        diagonals.reshape(packs, pack, whole),
        segments[:, :, None],
        segments[:, None, :],
        lse,
    )
    return gq, gk, gv, jnp.sum(gd, axis=0).reshape(packs * pack, whole)


def norm_back(grad_norm, value, inverse, gain):
    scaled = grad_norm * gain
    grad_value = inverse * scaled - value * inverse * inverse * inverse * jnp.mean(
        scaled * value, axis=-1, keepdims=True
    )
    return (grad_value, jnp.sum(grad_norm * value * inverse, axis=0))


def to_column(parts, rows):
    return jnp.pad(parts, ((0, 0), (0, rows - parts.shape[1]))).reshape(-1, 1)


def from_column(column, count, shape):
    return column.reshape(count, -1)[:, : shape[0] * shape[1]].reshape(count * shape[0], shape[1])


def exchange(blocks, count, sign):
    got = [blocks[0]]
    for step in range(1, count):
        pairs = [(item, (item + sign * step) % count) for item in range(count)]
        got.append(lax.ppermute(blocks[step], "expert", pairs))
    return jnp.stack(got)


def gelu_both(v):
    square = v * v
    t = jnp.tanh(0.7978845608028654 * (v + 0.044715 * v * square))
    half = 0.5 * (1.0 + t)
    slope = half + 0.5 * v * (1.0 - t * t) * (0.7978845608028654 * (1.0 + 0.134145 * square))
    return v * half, slope


def dot_nt(a, b):
    return lax.dot_general(a, b, (((1,), (1,)), ((), ())), preferred_element_type=jnp.float32)


def dot_nn(a, b):
    return jnp.dot(a, b, preferred_element_type=jnp.float32)


def expert_kernel(x_ref, g_ref, in_ref, out_ref, p_ref, a_ref, sum_p, sum_a):
    part = pl.program_id(1)
    width = x_ref.shape[-1]
    x = x_ref[...].reshape(-1, width)
    g = g_ref[...].reshape(-1, width)
    value, slope = gelu_both(dot_nt(x, in_ref[0]))
    grad_hidden = (dot_nt(g, out_ref[0]) * slope).astype(jnp.bfloat16)
    made = dot_nn(value.astype(jnp.bfloat16), out_ref[0])
    back = dot_nn(grad_hidden, in_ref[0])

    @pl.when(part == 0)
    def _():
        sum_p[...] = made
        sum_a[...] = back

    @pl.when(part > 0)
    def _():
        sum_p[...] += made
        sum_a[...] += back

    @pl.when(part == pl.num_programs(1) - 1)
    def _():
        p_ref[...] = sum_p[...].astype(jnp.bfloat16).reshape(p_ref.shape)
        a_ref[...] = sum_a[...].astype(jnp.bfloat16).reshape(a_ref.shape)


def expert_rows(arrived, grad_produced, w_in, w_out):
    count, experts, cap, width = arrived.shape
    hidden = w_in.shape[1]
    part = hidden // 3 if hidden % 3 == 0 else hidden
    rows_spec = pl.BlockSpec((count, 1, cap, width), lambda e, f: (0, e, 0, 0))
    weight_spec = pl.BlockSpec((1, part, width), lambda e, f: (e, f, 0))
    return pl.pallas_call(
        expert_kernel,
        grid=(experts, hidden // part),
        in_specs=[rows_spec, rows_spec, weight_spec, weight_spec],
        out_specs=[rows_spec, rows_spec],
        out_shape=[jax.ShapeDtypeStruct(arrived.shape, jnp.bfloat16)] * 2,
        scratch_shapes=[pltpu.VMEM((count * cap, width), jnp.float32)] * 2,
        compiler_params=pltpu.CompilerParams(vmem_limit_bytes=56 * 2**20),
        cost_estimate=pl.CostEstimate(
            flops=8 * count * experts * cap * width * hidden,
            bytes_accessed=4 * experts * hidden * width + 8 * arrived.size,
            transcendentals=count * experts * cap * hidden,
        ),
        name="expert_rows",
    )(arrived, grad_produced, w_in, w_out)


def weight_kernel(x_ref, g_ref, in_ref, out_ref, gi_ref, go_ref):
    step = pl.program_id(1)
    width = x_ref.shape[-1]
    x = x_ref[...].reshape(-1, width)
    g = g_ref[...].reshape(-1, width)
    value, slope = gelu_both(dot_nt(in_ref[0], x))
    grad_hidden = (dot_nt(out_ref[0], g) * slope).astype(jnp.bfloat16)
    for_in = dot_nn(grad_hidden, x)
    for_out = dot_nn(value.astype(jnp.bfloat16), g)

    @pl.when(step == 0)
    def _():
        gi_ref[0] = for_in
        go_ref[0] = for_out

    @pl.when(step > 0)
    def _():
        gi_ref[0] += for_in
        go_ref[0] += for_out


def expert_weight_grads(arrived_all, grad_all, w_in, w_out):
    dp_count, count, experts, cap, width = arrived_all.shape
    hidden = w_in.shape[1]
    many = max(1, min(dp_count, 1024 // (count * cap)))
    rows_spec = pl.BlockSpec((many, count, 1, cap, width), lambda e, r: (r, 0, e, 0, 0))
    weight_spec = pl.BlockSpec((1, hidden, width), lambda e, r: (e, 0, 0))
    return pl.pallas_call(
        weight_kernel,
        grid=(experts, dp_count // many),
        in_specs=[rows_spec, rows_spec, weight_spec, weight_spec],
        out_specs=[weight_spec, weight_spec],
        out_shape=[jax.ShapeDtypeStruct((experts, hidden, width), jnp.float32)] * 2,
        compiler_params=pltpu.CompilerParams(vmem_limit_bytes=56 * 2**20),
        cost_estimate=pl.CostEstimate(
            flops=8 * arrived_all.size * hidden,
            bytes_accessed=4 * arrived_all.size + 12 * w_in.size,
            transcendentals=arrived_all.size // width * hidden,
        ),
        name="expert_weight_grads",
    )(arrived_all, grad_all, w_in, w_out)


def on_device(
    inputs,
    gain_attn,
    w_query,
    w_key,
    w_value,
    w_output,
    bias_table,
    gain_ffn,
    w_router,
    w_in,
    w_out,
    segments,
    buckets,
    routes,
    slot_ids,
    cotangent,
):
    dp_count = lax.axis_size("dp")
    group_count = lax.axis_size("expert")
    group = lax.axis_index("expert")
    shard = lax.axis_index("dp")
    shard_rows, head_count = w_query.shape[0], bias_table.shape[1]
    expert_count = w_router.shape[1]
    bucket_count = bias_table.shape[0] * dp_count
    small = jnp.concatenate(
        [
            gain_attn[:, None],
            gain_ffn[:, None],
            to_column(bias_table.reshape(1, -1), shard_rows),
            w_router,
        ],
        axis=1,
    )
    small = jnp.pad(small, ((0, 0), (0, 128 - small.shape[1])))
    first_all = lax.all_gather(
        jnp.concatenate([w_query, w_key, w_value, small], axis=1), "dp", axis=0, tiled=True
    )
    output_weight = lax.all_gather(w_output, "dp", axis=0, tiled=True)
    attn_width = w_query.shape[1]
    qkv_weight = first_all[:, : 3 * attn_width]
    small_all = first_all[:, 3 * attn_width :]
    gain_attn_all = small_all[:, 0]
    gain_ffn_all = small_all[:, 1]
    table_all = from_column(small_all[:, 2], dp_count, bias_table.shape)
    router_weight = small_all[:, 3 : 3 + expert_count]
    token_count, model_width = inputs.shape
    head_size = attn_width // head_count

    bucket_pick = (
        jnp.arange(bucket_count, dtype=jnp.int32)[:, None] == diagonal_buckets(buckets)[None, :]
    ).astype(jnp.float32)
    diagonals = jnp.einsum(
        "bh,bm->hm", table_all.astype(jnp.float32), bucket_pick, precision=lax.Precision.HIGHEST
    )
    input_float = inputs.astype(jnp.float32)
    attn_gain = gain_attn_all.astype(jnp.float32)
    inverse_attn = lax.rsqrt(jnp.mean(input_float * input_float, axis=-1, keepdims=True) + epsilon)
    normed = (input_float * inverse_attn * attn_gain).astype(jnp.bfloat16)
    qkv = jnp.dot(normed, qkv_weight, preferred_element_type=jnp.float32).astype(jnp.bfloat16)
    attended, log_sums = attend(qkv, diagonals, segments, head_size)
    branch = jnp.dot(attended, output_weight, preferred_element_type=jnp.float32)
    middle = input_float + branch
    ffn_gain = gain_ffn_all.astype(jnp.float32)
    inverse_ffn = lax.rsqrt(jnp.mean(middle * middle, axis=-1, keepdims=True) + epsilon)
    normed2 = (middle * inverse_ffn * ffn_gain).astype(jnp.bfloat16)
    logits = jnp.dot(normed2, router_weight, preferred_element_type=jnp.float32)
    router_probs = jax.nn.softmax(logits, axis=-1)
    route_pick = (routes[:, None] == jnp.arange(expert_count, dtype=jnp.int32)[None, :]).astype(
        jnp.float32
    )
    gate_value = jnp.sum(router_probs * route_pick, axis=-1)
    local_experts = expert_count // group_count
    turn = lax.rem(routes // local_experts - group + group_count, group_count)
    slot_place = (turn * local_experts + lax.rem(routes, local_experts)) * CAP + slot_ids
    dispatch = (
        slot_place[:, None] == jnp.arange(expert_count * CAP, dtype=jnp.int32)[None, :]
    ).astype(jnp.bfloat16)
    block_shape = (group_count, local_experts, CAP, model_width)

    def to_slots(rows):
        return (
            jnp.einsum("ts,td->sd", dispatch, rows, preferred_element_type=jnp.float32)
            .astype(jnp.bfloat16)
            .reshape(block_shape)
        )

    def from_slots(blocks):
        return jnp.dot(
            dispatch,
            blocks.reshape(expert_count * CAP, model_width),
            preferred_element_type=jnp.float32,
        )

    grad_out = cotangent.astype(jnp.float32)
    grad_back = (gate_value[:, None] * grad_out).astype(jnp.bfloat16)
    arrived = exchange(to_slots(normed2), group_count, 1)
    grad_produced = exchange(to_slots(grad_back), group_count, 1)
    arrived_all = lax.all_gather(arrived, "dp", axis=0)
    grad_produced_all = lax.all_gather(grad_produced, "dp", axis=0)
    produced, grad_arrived = expert_rows(arrived, grad_produced, w_in, w_out)
    returned = from_slots(exchange(produced, group_count, -1))
    grad_normed2 = from_slots(exchange(grad_arrived, group_count, -1))
    output = (middle + gate_value[:, None] * returned).astype(jnp.bfloat16)
    grad_gate = jnp.sum(grad_out * returned, axis=-1)
    hidden_part = w_in.shape[1] // dp_count
    grad_w_in, grad_w_out = expert_weight_grads(
        arrived_all,
        grad_produced_all,
        lax.dynamic_slice_in_dim(w_in, shard * hidden_part, hidden_part, 1),
        lax.dynamic_slice_in_dim(w_out, shard * hidden_part, hidden_part, 1),
    )
    grad_probs = route_pick * grad_gate[:, None]
    grad_logits = (
        router_probs * (grad_probs - jnp.sum(router_probs * grad_probs, axis=-1, keepdims=True))
    ).astype(jnp.bfloat16)
    router_local = jnp.einsum("td,te->de", normed2, grad_logits, preferred_element_type=jnp.float32)
    grad_normed2 = grad_normed2 + jnp.einsum(
        "te,de->td", grad_logits, router_weight, preferred_element_type=jnp.float32
    )
    grad_mid_norm, ffn_gain_local = norm_back(grad_normed2, middle, inverse_ffn, ffn_gain)
    grad_middle = grad_out + grad_mid_norm
    grad_branch = grad_middle.astype(jnp.bfloat16)
    output_local = jnp.einsum(
        "tc,td->cd", attended, grad_branch, preferred_element_type=jnp.float32
    )
    grad_attended = jnp.einsum(
        "td,cd->tc", grad_branch, output_weight, preferred_element_type=jnp.float32
    ).astype(jnp.bfloat16)
    grad_q_rows, grad_k_rows, grad_v_rows, grad_diagonals = attend_back(
        qkv, grad_attended, diagonals, segments, log_sums, head_size
    )
    table_local = jnp.einsum(
        "bm,hm->bh", bucket_pick, grad_diagonals, precision=lax.Precision.HIGHEST
    )
    grad_qkv = jnp.concatenate([grad_q_rows, grad_k_rows, grad_v_rows], axis=1)
    qkv_local = jnp.einsum("td,tc->dc", normed, grad_qkv, preferred_element_type=jnp.float32)
    grad_normed = jnp.einsum("tc,dc->td", grad_qkv, qkv_weight, preferred_element_type=jnp.float32)
    grad_in_norm, attn_gain_local = norm_back(grad_normed, input_float, inverse_attn, attn_gain)
    grad_inputs = (grad_middle + grad_in_norm).astype(jnp.bfloat16)
    packed = jnp.concatenate(
        [
            qkv_local,
            output_local,
            attn_gain_local[:, None],
            ffn_gain_local[:, None],
            to_column(table_local.reshape(dp_count, -1), shard_rows),
            router_local,
        ],
        axis=1,
    ).astype(jnp.bfloat16)
    packed = jnp.pad(packed, ((0, 0), (0, -packed.shape[1] % 128)))
    packed = lax.psum_scatter(packed, "dp", scatter_dimension=0, tiled=True)
    packed = lax.psum(packed, "expert").astype(jnp.float32)
    grad_w_query = packed[:, :attn_width]
    grad_w_key = packed[:, attn_width : 2 * attn_width]
    grad_w_value = packed[:, 2 * attn_width : 3 * attn_width]
    grad_w_output = packed[:, 3 * attn_width : 3 * attn_width + model_width]
    rest = packed[:, 3 * attn_width + model_width :]
    grad_gain_attn = rest[:, 0]
    grad_gain_ffn = rest[:, 1]
    grad_bias_table = rest[: bias_table.size, 2].reshape(bias_table.shape)
    grad_w_router = rest[:, 3 : 3 + expert_count]
    return (
        output,
        grad_inputs,
        grad_gain_attn,
        grad_w_query,
        grad_w_key,
        grad_w_value,
        grad_w_output,
        grad_bias_table,
        grad_gain_ffn,
        grad_w_router,
        grad_w_in,
        grad_w_out,
    )


def solution(mesh):
    placed = (
        P(("expert", "dp"), None),
        P("dp"),
        P("dp", None),
        P("dp", None),
        P("dp", None),
        P("dp", None),
        P("dp", None),
        P("dp"),
        P("dp", None),
        P("expert", None, None),
        P("expert", None, None),
        P(("expert", "dp"), None),
        P(),
        P(("expert", "dp")),
        P(("expert", "dp")),
        P(("expert", "dp"), None),
    )
    return jax.shard_map(
        on_device,
        mesh=mesh,
        in_specs=placed,
        out_specs=(
            P(("expert", "dp"), None),
            P(("expert", "dp"), None),
            P("dp"),
            P("dp", None),
            P("dp", None),
            P("dp", None),
            P("dp", None),
            P("dp", None),
            P("dp"),
            P("dp", None),
            P("expert", "dp", None),
            P("expert", "dp", None),
        ),
        check_vma=False,
    )
```

time: 1770 us -> 1030 us (0.58)
  matrix products: 467 us -> 49 us
  Pallas kernels: 0 us -> 202 us
  blocking collectives: 163 us -> 0 us
  waiting for transfers between devices: 822 us -> 672 us
  local copies, waits for them, and re-layouts: 164 us -> 51.8 us
  other arithmetic: 103 us -> 18.9 us
    reduce_scatter x6 -> x1, waiting for transfers between devices: 769 us -> 55.5 us  [on_device(): packed = lax.psum_scatter(packed, 'dp', scatter_dimension=0, tiled=True)]
    all_gather x4, waiting for transfers between devices: 0.04 us -> 472 us  [the longest x1 220 us: on_device(): grad_produced_all = lax.all_gather(grad_produced, 'dp', axis=0)]
    dot_general x37 -> x9, matrix products: 452 us -> 37.3 us  [the longest x2 8.8 us: to_slots(): jnp.einsum('ts,td->sd', dispatch, rows, preferred_element_type=jnp.float32)]
    pallas_call x0 -> x4, Pallas kernels: none -> 202 us  [the longest x1 59.1 us: attend_back(): pl.pallas_call(functools.partial(attend_back_kernel, size, 256), grid=spe...]
    ppermute x0 -> x12, waiting for transfers between devices: none -> 112 us  [exchange(): got.append(lax.ppermute(blocks[step], 'expert', pairs))]
    all_to_all x2 -> x0, blocking collectives: 79.8 us -> none  [the longest x1 41 us: on_device(): lax.all_to_all(sent_rows, 'expert', split_axis=0, concat_axis=1, tiled=True)]
    convert_element_type x16 -> x1, other arithmetic: 67.3 us -> 1.15 us  [on_device(): packed = lax.psum(packed, 'expert').astype(jnp.float32)]
    convert_element_type x5 -> x0, local copies, waits for them, and re-layouts: 56.5 us -> none  [the longest x2 45.9 us: step(): grad_scores = (attn_probs * (grad_weights - prob_dot)).astype(jnp.bfloat16)]
  transfers between devices with their start and end apart: 14 -> 18, of which waited for: 7 -> 12; matrix products, arithmetic and copies ran while one was open for 32% -> 5% of each run, Pallas kernels for 0% -> 4%
where the time goes in v1:
time: 1030 us; the launch traced here: 1020 us
  waiting for transfers between devices  672 us (65%)
  Pallas kernels  202 us (20%)
  local copies, waits for them, and re-layouts  51.8 us (5%)
  matrix products  49 us (5%)
  other arithmetic  18.9 us (2%)
  starting transfers between devices  15.2 us (1%)
  between operations  15 us (1%)
    all_gather x1, waiting for transfers between devices, on_device(): grad_produced_all = lax.all_gather(grad_produced, 'dp', axis=0)  220 us
    all_gather x1, waiting for transfers between devices, on_device(): arrived_all = lax.all_gather(arrived, 'dp', axis=0)  215 us
    ppermute x12, waiting for transfers between devices, exchange(): got.append(lax.ppermute(blocks[step], 'expert', pairs))  112 us
    pallas_call x1, Pallas kernels, attend_back(): pl.pallas_call(functools.partial(attend_back_kernel, size, 256), grid=spe...  59.1 us
    reduce_scatter x1, waiting for transfers between devices, on_device(): packed = lax.psum_scatter(packed, 'dp', scatter_dimension=0, tiled=True)  55.5 us
    pallas_call x1, Pallas kernels, expert_rows(): pl.pallas_call(expert_kernel, grid=(experts, hidden // part), in_specs=[r...  53.4 us
    pallas_call x1, Pallas kernels, expert_weight_grads(): pl.pallas_call(weight_kernel, grid=(experts, dp_count // many), in_specs=...  51.4 us
    pallas_call x1, Pallas kernels, attend(): pl.pallas_call(functools.partial(attend_kernel, size, 256), grid=specs['g...  37.7 us
  transfers between devices with their start and end apart: 18, of which 12 were waited for; matrix products, arithmetic and copies ran while one was open for 5% of the time, Pallas kernels for 4%

profile of v1, /device:TPU:0, one launch (start us, length us, event | category | flops | bytes accessed | tf_op | source)
XLA Modules:
  0.0 1023.8 jit_solution(14559612779349474278)
XLA Ops:
  19.2 37.5 %all-gather.7.cloned.1.call-done = bf16[768,2432]{1,0:T(8,128)(2,1)} async-done(((bf16[96,2432]{1,0:T(8,128)(2,1)}), bf16[768,2432]{1,0:T(8,128)(2,1)}) %all-gather.7.cloned.1.call-update) | async-done | bytes 3735568 | tf_op jit(solution)/shard_map/all_gather | solution.py:364
  60.4 7.8 convolution_convert_fusion.q_ref.k_ref.v_ref
  68.1 37.7 %attend.1 = (bf16[1024,768]{1,0:T(8,128)(2,1)}, f32[1,6,1024,2]{3,2,1,0:T(8,128)}) custom-call(bf16[1024,2304]{1,0:T(8,128)(2,1)} %convolution_convert_fusion.q_ref.k_ref.v_ref, bf16[1024,2304]{1,0:T(8,128)(2,1)} %convolution_convert_fusion.q_ref.k_ref.v_ref, bf16[1024,2304]{1,0:T(8,128)(2,1)} %convolution_convert_fusion.q_ref.k_ref.v_ref, ...), custom_call_target="tpu_custom_call" | custom-call | flops 12884901888 | bytes 23592960 | tf_op jit(solution)/shard_map/attend/pallas_call | solution.py:134
  105.9 3.4 multiply_reduce_fusion.2
  109.6 4.6 fusion.13
  119.6 4.2 fusion.16
  129.3 5.6 collective-permute-done.2
  137.3 16.8 %collective-permute-done.1 = bf16[8,64,768]{2,1,0:T(8,128)(2,1)S(1)} collective-permute-done((bf16[8,64,768]{2,1,0:T(8,128)(2,1)S(1)}, bf16[8,64,768]{2,1,0:T(8,128)(2,1)S(1)}, u32[]{:S(2)}, u32[]{:S(2)}) %collective-permute-start.1) | collective-permute-done | bytes 786464 | tf_op jit(solution)/shard_map/ppermute | solution.py:217
  156.0 12.7 %collective-permute-done.5 = bf16[8,64,768]{2,1,0:T(8,128)(2,1)} collective-permute-done((bf16[8,64,768]{2,1,0:T(8,128)(2,1)}, bf16[8,64,768]{2,1,0:T(8,128)(2,1)}, u32[]{:S(2)}, u32[]{:S(2)}) %collective-permute-start.5) | collective-permute-done | bytes 786464 | tf_op jit(solution)/shard_map/ppermute | solution.py:217
  168.8 18.2 %collective-permute-done.4 = bf16[8,64,768]{2,1,0:T(8,128)(2,1)} collective-permute-done((bf16[8,64,768]{2,1,0:T(8,128)(2,1)}, bf16[8,64,768]{2,1,0:T(8,128)(2,1)}, u32[]{:S(2)}, u32[]{:S(2)}) %collective-permute-start.4) | collective-permute-done | bytes 786464 | tf_op jit(solution)/shard_map/ppermute | solution.py:217
  187.0 3.2 pad_maximum_fusion.1.g_ref
  190.2 53.4 %expert_rows.1 = (bf16[4,8,64,768]{3,2,1,0:T(8,128)(2,1)}, bf16[4,8,64,768]{3,2,1,0:T(8,128)(2,1)}) custom-call(bf16[4,8,64,768]{3,2,1,0:T(8,128)(2,1)} %pad_maximum_fusion.x_ref, bf16[4,8,64,768]{3,2,1,0:T(8,128)(2,1)} %pad_maximum_fusion.1.g_ref, bf16[8,3072,768]{2,1,0:T(8,128)(2,1)} %in_ref.1, bf16[8,3072,768]{2,1,0:T(8,128)(2,1)} %out_ref.1), custom_call_target="tpu_custom_call" | custom-call | flops 38654705664 | bytes 88080384 | tf_op jit(solution)/shard_map/expert_rows/pallas_call | solution.py:269
  251.2 16.1 %collective-permute-done.8 = bf16[8,64,768]{2,1,0:T(8,128)(2,1)S(1)} collective-permute-done((bf16[8,64,768]{2,1,0:T(8,128)(2,1)S(1)}, bf16[8,64,768]{2,1,0:T(8,128)(2,1)S(1)}, u32[]{:S(2)}, u32[]{:S(2)}) %collective-permute-start.8) | collective-permute-done | bytes 786464 | tf_op jit(solution)/shard_map/ppermute | solution.py:217
  267.3 30.1 %collective-permute-done.7 = bf16[8,64,768]{2,1,0:T(8,128)(2,1)S(1)} collective-permute-done((bf16[8,64,768]{2,1,0:T(8,128)(2,1)S(1)}, bf16[8,64,768]{2,1,0:T(8,128)(2,1)S(1)}, u32[]{:S(2)}, u32[]{:S(2)}) %collective-permute-start.7) | collective-permute-done | bytes 786464 | tf_op jit(solution)/shard_map/ppermute | solution.py:217
  297.9 4.0 fusion.26
  303.1 12.3 %collective-permute-done.10 = bf16[8,64,768]{2,1,0:T(8,128)(2,1)S(1)} collective-permute-done((bf16[8,64,768]{2,1,0:T(8,128)(2,1)S(1)}, bf16[8,64,768]{2,1,0:T(8,128)(2,1)S(1)}, u32[]{:S(2)}, u32[]{:S(2)}) %collective-permute-start.10) | collective-permute-done | bytes 786464 | tf_op jit(solution)/shard_map/ppermute | solution.py:217
  319.4 4.8 multiply_reduce_fusion
  324.2 3.0 convert_add_fusion.1
  327.2 2.5 convolution_convert_fusion.3
  329.7 2.6 convolution_convert_fusion.2.grad_ref
  332.3 59.1 %attend_back.1 = (bf16[1024,768]{1,0:T(8,128)(2,1)}, bf16[1024,768]{1,0:T(8,128)(2,1)}, bf16[1024,768]{1,0:T(8,128)(2,1)}, f32[1,6,2,2048]{3,2,1,0:T(2,128)}) custom-call(bf16[1024,2304]{1,0:T(8,128)(2,1)} %convolution_convert_fusion.q_ref.k_ref.v_ref, bf16[1024,2304]{1,0:T(8,128)(2,1)} %convolution_convert_fusion.q_ref.k_ref.v_ref, ...), custom_call_target="tpu_custom_call" | custom-call | flops 32212254720 | bytes 37748736 | tf_op jit(solution)/shard_map/attend_back/pallas_call | solution.py:166
  393.9 5.7 convolution_convert_fusion.1
  399.6 5.8 fusion.30
  407.6 8.2 concatenate.20
  415.8 5.0 pad.20
  420.9 55.5 %reduce-scatter.2.cloned.1.call-done = bf16[96,3200]{1,0:T(8,128)(2,1)} async-done(((bf16[768,3200]{1,0:T(8,128)(2,1)}), bf16[96,3200]{1,0:T(8,128)(2,1)}) %reduce-scatter.2.cloned.1.call-update) | async-done | bytes 614416 | tf_op jit(solution)/shard_map/reduce_scatter | solution.py:481
  477.6 8.4 constant_dynamic-slice_fusion
  487.6 3.9 fusion.24
  493.1 31.0 %all-reduce.6.cloned.1.call-done = bf16[96,3200]{1,0:T(8,128)(2,1)} async-done(((bf16[96,3200]{1,0:T(8,128)(2,1)}), bf16[96,3200]{1,0:T(8,128)(2,1)}) %all-reduce.6.cloned.1.call-update) | async-done | bytes 614416 | tf_op jit(solution)/shard_map/psum | solution.py:482
  530.5 215.2 %all-gather.11.cloned.1.call-done = bf16[32,8,64,768]{3,2,1,0:T(8,128)(2,1)} async-done(((bf16[4,8,64,768]{3,2,1,0:T(8,128)(2,1)}), bf16[32,8,64,768]{3,2,1,0:T(8,128)(2,1)}) %all-gather.11.cloned.1.call-update) | async-done | bytes 25165840 | tf_op jit(solution)/shard_map/all_gather | solution.py:427
  745.6 219.6 %all-gather.13.cloned.1.call-done = bf16[32,8,64,768]{3,2,1,0:T(8,128)(2,1)} async-done(((bf16[4,8,64,768]{3,2,1,0:T(8,128)(2,1)}), bf16[32,8,64,768]{3,2,1,0:T(8,128)(2,1)}) %all-gather.13.cloned.1.call-update) | async-done | bytes 25165840 | tf_op jit(solution)/shard_map/all_gather | solution.py:428
  965.2 51.4 %expert_weight_grads.1 = (f32[8,384,768]{2,1,0:T(8,128)}, f32[8,384,768]{2,1,0:T(8,128)}) custom-call(bf16[8,4,8,64,768]{4,3,2,1,0:T(8,128)(2,1)} %bitcast.87, bf16[8,4,8,64,768]{4,3,2,1,0:T(8,128)(2,1)} %bitcast.88, bf16[8,384,768]{2,1,0:T(8,128)(2,1)} %get-tuple-element.119.in_ref, bf16[8,384,768]{2,1,0:T(8,128)(2,1)} %get-tuple-element.118.out_ref), custom_call_target="tpu_custom_call" | custom-call | flops 38654705664 | bytes 78643200 | tf_op jit(solution)/shard_map/expert_weight_grads/pallas_call | solution.py:313
  (130 shorter events, 59.5 us)
Async XLA Ops:
  7.2 49.5 %all-gather.7.cloned.1.call-start = ((), (), s32[]{:S(2)}) async-start(), calls=%async_computation.1 | async-start | bytes 4202496 | tf_op jit(solution)/shard_map/all_gather | solution.py:364
  10.7 95.1 %all-gather.9.cloned.1.call-start = ((), (), s32[]{:S(2)}) async-start(), calls=%async_computation.2 | async-start | bytes 1327104 | tf_op jit(solution)/shard_map/all_gather | solution.py:367
  11.5 465.0 %reduce-scatter.2.cloned.1.call-start = ((), (), s32[]{:S(2)}) async-start(), calls=%async_computation.3 | async-start | bytes 5529600 | tf_op jit(solution)/shard_map/reduce_scatter | solution.py:481
  15.3 3.2 slice-start
  15.3 3.9 copy-start.14
  15.3 3.9 copy-start.16
  19.2 48.9 %copy-start.12 = (s32[2048]{0:T(1024)}, s32[2048]{0:T(1024)S(1)}, u32[]{:S(2)}) copy-start(s32[2048]{0:T(1024)S(1)} %concatenate.18) | copy-start | bytes 24580
  109.3 5.0 copy-start.1
  109.6 8.4 copy-start.4
  114.5 20.4 %collective-permute-start.2 = (bf16[8,64,768]{2,1,0:T(8,128)(2,1)S(1)}, bf16[8,64,768]{2,1,0:T(8,128)(2,1)S(1)}, u32[]{:S(2)}, u32[]{:S(2)}) collective-permute-start(bf16[8,64,768]{2,1,0:T(8,128)(2,1)S(1)} %bitcast.75), channel_id=1, source_target_pairs={{0,24},{8,0},{16,8},{24,16},{1,25},{9,1},{17,9},{25,17},{2,26},{10... | collective-permute-start | bytes 2359304 | tf_op jit(solution)/shard_map/ppermute | solution.py:217
  116.9 37.3 %collective-permute-start.1 = (bf16[8,64,768]{2,1,0:T(8,128)(2,1)S(1)}, bf16[8,64,768]{2,1,0:T(8,128)(2,1)S(1)}, u32[]{:S(2)}, u32[]{:S(2)}) collective-permute-start(bf16[8,64,768]{2,1,0:T(8,128)(2,1)S(1)} %bitcast.69), channel_id=1, source_target_pairs={{0,16},{8,24},{16,0},{24,8},{1,17},{9,25},{17,1},{25,9},{2,18},{10... | collective-permute-start | bytes 2359304 | tf_op jit(solution)/shard_map/ppermute | solution.py:217
  117.5 36.7 %collective-permute-start = (bf16[8,64,768]{2,1,0:T(8,128)(2,1)S(1)}, bf16[8,64,768]{2,1,0:T(8,128)(2,1)S(1)}, u32[]{:S(2)}, u32[]{:S(2)}) collective-permute-start(bf16[8,64,768]{2,1,0:T(8,128)(2,1)S(1)} %bitcast.66), channel_id=1, source_target_pairs={{0,8},{8,16},{16,24},{24,0},{1,9},{9,17},{17,25},{25,1},{2,10},{10... | collective-permute-start | bytes 2359304 | tf_op jit(solution)/shard_map/ppermute | solution.py:217
  125.5 43.3 %collective-permute-start.5 = (bf16[8,64,768]{2,1,0:T(8,128)(2,1)}, bf16[8,64,768]{2,1,0:T(8,128)(2,1)}, u32[]{:S(2)}, u32[]{:S(2)}) collective-permute-start(bf16[8,64,768]{2,1,0:T(8,128)(2,1)} %bitcast.22), channel_id=1, source_target_pairs={{0,24},{8,0},{16,8},{24,16},{1,25},{9,1},{17,9},{25,17},{2,26},{10... | collective-permute-start | bytes 2359304 | tf_op jit(solution)/shard_map/ppermute | solution.py:217
  127.8 59.2 %collective-permute-start.4 = (bf16[8,64,768]{2,1,0:T(8,128)(2,1)}, bf16[8,64,768]{2,1,0:T(8,128)(2,1)}, u32[]{:S(2)}, u32[]{:S(2)}) collective-permute-start(bf16[8,64,768]{2,1,0:T(8,128)(2,1)} %bitcast.20), channel_id=1, source_target_pairs={{0,16},{8,24},{16,0},{24,8},{1,17},{9,25},{17,1},{25,9},{2,18},{10... | collective-permute-start | bytes 2359304 | tf_op jit(solution)/shard_map/ppermute | solution.py:217
  134.9 52.1 %collective-permute-start.3 = (bf16[8,64,768]{2,1,0:T(8,128)(2,1)}, bf16[8,64,768]{2,1,0:T(8,128)(2,1)}, u32[]{:S(2)}, u32[]{:S(2)}) collective-permute-start(bf16[8,64,768]{2,1,0:T(8,128)(2,1)} %bitcast.18), channel_id=1, source_target_pairs={{0,8},{8,16},{16,24},{24,0},{1,9},{9,17},{17,25},{25,1},{2,10},{10... | collective-permute-start | bytes 2359304 | tf_op jit(solution)/shard_map/ppermute | solution.py:217
  243.6 5.8 copy-start.6
  245.9 21.4 %collective-permute-start.8 = (bf16[8,64,768]{2,1,0:T(8,128)(2,1)S(1)}, bf16[8,64,768]{2,1,0:T(8,128)(2,1)S(1)}, u32[]{:S(2)}, u32[]{:S(2)}) collective-permute-start(bf16[8,64,768]{2,1,0:T(8,128)(2,1)S(1)} %get-tuple-element.95), channel_id=1, source_target_pairs={{0,8},{8,16},{16,24},{24,0},{1,9},{9,17},{17,25},{25,1},{2,10},{10... | collective-permute-start | bytes 2359304 | tf_op jit(solution)/shard_map/ppermute | solution.py:217
  246.3 51.1 %collective-permute-start.7 = (bf16[8,64,768]{2,1,0:T(8,128)(2,1)S(1)}, bf16[8,64,768]{2,1,0:T(8,128)(2,1)S(1)}, u32[]{:S(2)}, u32[]{:S(2)}) collective-permute-start(bf16[8,64,768]{2,1,0:T(8,128)(2,1)S(1)} %get-tuple-element.96), channel_id=1, source_target_pairs={{0,16},{8,24},{16,0},{24,8},{1,17},{9,25},{17,1},{25,9},{2,18},{10... | collective-permute-start | bytes 2359304 | tf_op jit(solution)/shard_map/ppermute | solution.py:217
  247.1 50.4 %collective-permute-start.6 = (bf16[8,64,768]{2,1,0:T(8,128)(2,1)S(1)}, bf16[8,64,768]{2,1,0:T(8,128)(2,1)S(1)}, u32[]{:S(2)}, u32[]{:S(2)}) collective-permute-start(bf16[8,64,768]{2,1,0:T(8,128)(2,1)S(1)} %get-tuple-element.97), channel_id=1, source_target_pairs={{0,24},{8,0},{16,8},{24,16},{1,25},{9,1},{17,9},{25,17},{2,26},{10... | collective-permute-start | bytes 2359304 | tf_op jit(solution)/shard_map/ppermute | solution.py:217
  249.6 53.5 %collective-permute-start.11 = (bf16[8,64,768]{2,1,0:T(8,128)(2,1)S(1)}, bf16[8,64,768]{2,1,0:T(8,128)(2,1)S(1)}, u32[]{:S(2)}, u32[]{:S(2)}) collective-permute-start(bf16[8,64,768]{2,1,0:T(8,128)(2,1)S(1)} %get-tuple-element.91), channel_id=1, source_target_pairs={{0,8},{8,16},{16,24},{24,0},{1,9},{9,17},{17,25},{25,1},{2,10},{10... | collective-permute-start | bytes 2359304 | tf_op jit(solution)/shard_map/ppermute | solution.py:217
  249.7 65.7 %collective-permute-start.10 = (bf16[8,64,768]{2,1,0:T(8,128)(2,1)S(1)}, bf16[8,64,768]{2,1,0:T(8,128)(2,1)S(1)}, u32[]{:S(2)}, u32[]{:S(2)}) collective-permute-start(bf16[8,64,768]{2,1,0:T(8,128)(2,1)S(1)} %get-tuple-element.92), channel_id=1, source_target_pairs={{0,16},{8,24},{16,0},{24,8},{1,17},{9,25},{17,1},{25,9},{2,18},{10... | collective-permute-start | bytes 2359304 | tf_op jit(solution)/shard_map/ppermute | solution.py:217
  267.3 48.1 %collective-permute-start.9 = (bf16[8,64,768]{2,1,0:T(8,128)(2,1)S(1)}, bf16[8,64,768]{2,1,0:T(8,128)(2,1)S(1)}, u32[]{:S(2)}, u32[]{:S(2)}) collective-permute-start(bf16[8,64,768]{2,1,0:T(8,128)(2,1)S(1)} %get-tuple-element.93), channel_id=1, source_target_pairs={{0,24},{8,0},{16,8},{24,16},{1,25},{9,1},{17,9},{25,17},{2,26},{10... | collective-permute-start | bytes 2359304 | tf_op jit(solution)/shard_map/ppermute | solution.py:217
  297.9 4.1 copy-start.5
  324.2 3.0 copy-start.18
  327.2 2.5 copy-start
  399.6 6.2 copy-start.11
  399.6 6.3 copy-start.13
  399.6 8.0 copy-start.9
  420.9 103.3 %all-reduce.6.cloned.1.call-start = ((), (), s32[]{:S(2)}) async-start(), calls=%async_computation.4 | async-start | bytes 1228800 | tf_op jit(solution)/shard_map/psum | solution.py:482
  476.5 269.2 %all-gather.11.cloned.1.call-start = ((), (), s32[]{:S(2)}) async-start(), calls=%async_computation.5 | async-start | bytes 28311552 | tf_op jit(solution)/shard_map/all_gather | solution.py:427
  477.0 488.2 %all-gather.13.cloned.1.call-start = ((), (), s32[]{:S(2)}) async-start(), calls=%async_computation.6 | async-start | bytes 28311552 | tf_op jit(solution)/shard_map/all_gather | solution.py:428
  477.6 8.4 copy-start.3
  (6 other events, 12.8 us)
Sparse Core Ops, SparseCore 0:
  10.8 45.8 all-gather.6
  58.4 21.5 all-gather.8
  421.0 55.4 reduce-scatter.1
  479.3 44.7 all-reduce.5
  525.6 219.9 all-gather.10
  747.1 218.0 all-gather.12
